TPU v7x, 512 devices: a whole 4x8x8 slice. The times are simulated.
512 devices in a mesh: row: 32 (over z, x), col: 16 (over y, core).
Axes of the slice: x: 4, y: 8, z: 8, core: 2. Of those that a mesh axis runs over, the one named last changes fastest.
Arguments:
- density: float32 [32, 256, 2048], P(None, 'row', 'col'), may hold values from 0 to 1
- threshold_index: int32 [3], replicated, may hold values from 4 to 12
- channel_width: int32 [30], replicated, may hold values from 0 to 9
- sigma_table: float32 [10], replicated, may hold values from 1.5 to 64
Outputs:
- compliance: float32 [30], replicated
- sensitivity: float32 [32, 256, 2048], P(None, 'row', 'col')
All inputs are finite; a program needn't handle non-finite values.
Results may differ from a plain program's by a relative error of at most 0.0013.
Values may be sent and summed in bfloat16 or wider, within the bound.
No kernel may reach another device: no remote copies, remote signals or barrier semaphores. Data moves between devices by JAX's collectives and lax.ppermute only.
A program may use at most 64 MiB of HBM per device.

v0:
```python
from functools import partial
import jax
import jax.numpy as jnp
from jax import lax
from jax.sharding import PartitionSpec as P

VARIANTS = 3
WIDTHS = 10
CHANNELS = 30
HALF = 128
sharpness = 8.0
spread_floor = 0.0001


def extended(x, sides, width):
    for axis, dim in sides:
        size, length = (lax.axis_size(axis), x.shape[dim])
        up = [(i, (i + 1) % size) for i in range(size - 1)]
        down = [(j, i) for i, j in up]
        last = lax.slice_in_dim(x, length - width, length, axis=dim)
        first = lax.slice_in_dim(x, 0, width, axis=dim)
        before = lax.ppermute(last, axis, up)
        after = lax.ppermute(first, axis, down)
        x = jnp.concatenate([before, x, after], axis=dim)
    return x


def project(density, threshold_index):
    levels = threshold_index.astype(jnp.float32) / 16.0
    levels = levels.reshape((-1,) + (1,) * density.ndim)
    low = jnp.tanh(sharpness * levels)
    high = jnp.tanh(sharpness * (1.0 - levels))
    return (low + jnp.tanh(sharpness * (density - levels))) / (low + high)


def slope(density, threshold_index):
    levels = threshold_index.astype(jnp.float32) / 16.0
    levels = levels.reshape((-1,) + (1,) * density.ndim)
    low = jnp.tanh(sharpness * levels)
    high = jnp.tanh(sharpness * (1.0 - levels))
    inner = jnp.tanh(sharpness * (density - levels))
    return sharpness * (1.0 - inner * inner) / (low + high)


def gauss_band(width_value, num_rows, num_cols, offset):
    row_ids = lax.broadcasted_iota(jnp.float32, (num_rows, num_cols), 0)
    col_ids = lax.broadcasted_iota(jnp.float32, (num_rows, num_cols), 1)
    offsets = row_ids - col_ids - offset
    tap_axis = jnp.arange(-HALF, HALF + 1).astype(jnp.float32)
    inverse = 1.0 / jnp.sum(jnp.exp(-tap_axis * tap_axis / (2.0 * width_value * width_value)))
    values = jnp.exp(-offsets * offsets / (2.0 * width_value * width_value)) * inverse
    return jnp.where(jnp.abs(offsets) <= HALF, values, 0.0).astype(jnp.bfloat16)


def width_of(sigma_table, channel_width, index):
    slot = jnp.sum(jnp.where(jnp.arange(channel_width.shape[0]) == index, channel_width, 0))
    return jnp.sum(jnp.where(jnp.arange(sigma_table.shape[0]) == slot, sigma_table, 0.0))


def along_x(sigma_table, channel_width, wide, index):
    variant = index // WIDTHS
    cols_out = wide.shape[-1] - 2 * HALF
    matrix = gauss_band(
        width_of(sigma_table, channel_width, index), wide.shape[-1], cols_out, float(HALF)
    )
    source = lax.dynamic_index_in_dim(wide, variant, 0, keepdims=False)
    return jnp.einsum("...j,ji->...i", source, matrix, preferred_element_type=jnp.float32).astype(
        jnp.bfloat16
    )


def per_device(density, threshold_index, channel_width, sigma_table):
    channel_ids = jnp.arange(CHANNELS, dtype=jnp.int32)
    smooth_x = partial(along_x, sigma_table, channel_width)
    wide_density = extended(density, (("col", 2),), HALF)
    wide = project(wide_density, threshold_index).astype(jnp.bfloat16)
    panels = lax.map(partial(smooth_x, wide), channel_ids)
    middle = wide[..., HALF : wide.shape[-1] - HALF]
    panels, variants = (
        lax.all_to_all(panels, "row", split_axis=1, concat_axis=2, tiled=True),
        lax.all_to_all(middle, "row", split_axis=1, concat_axis=2, tiled=True),
    )
    length = variants.shape[2]

    def along_y(index):
        variant = index // WIDTHS
        matrix = gauss_band(width_of(sigma_table, channel_width, index), length, length, 0.0)
        source = lax.dynamic_index_in_dim(panels, index, 0, keepdims=False)
        field = jnp.einsum("zyx,yw->zwx", source, matrix, preferred_element_type=jnp.float32)
        owner = lax.dynamic_index_in_dim(variants, variant, 0, keepdims=False).astype(jnp.float32)
        return (field, jnp.sum(owner * field))

    smoothed, partials = lax.map(along_y, channel_ids)
    cell_count = (
        lax.axis_size("row") * lax.axis_size("col") * variants.shape[1] * length * variants.shape[3]
    )
    compliance = lax.psum(partials, ("row", "col")) / cell_count
    mean_value = jnp.mean(compliance)
    spread = jnp.sqrt(jnp.mean((compliance - mean_value) ** 2) + spread_floor)
    weights = (1.0 + (compliance - mean_value) / spread) / CHANNELS
    member = (
        lax.broadcasted_iota(jnp.int32, (VARIANTS, CHANNELS), 1) // WIDTHS
        == lax.broadcasted_iota(jnp.int32, (VARIANTS, CHANNELS), 0)
    ).astype(jnp.float32)
    combined = jnp.einsum(
        "vc,czyx->vzyx",
        member * (2.0 * weights)[None, :],
        smoothed,
        precision=lax.Precision.HIGHEST,
    )
    returned = lax.all_to_all(combined, "row", split_axis=2, concat_axis=1, tiled=True)
    sensitivity = jnp.sum(slope(density, threshold_index) * returned, axis=0)
    return (compliance, sensitivity)


def solution(mesh):
    in_specs = (P(None, "row", "col"), P(), P(), P())
    out_specs = (P(), P(None, "row", "col"))
    return jax.shard_map(
        per_device, mesh=mesh, in_specs=in_specs, out_specs=out_specs, check_vma=False
    )
```

profile of v0, /device:TPU:16, one launch (start us, length us, event | category | flops | bytes accessed | tf_op | source)
XLA Modules:
  0.0 859.1 jit_solution(10198214440540660656)
XLA Ops:
  0.6 2.1 collective-permute-start
  2.7 3.6 collective-permute-start.1
  7.3 1.9 collective-permute-done.1
  11.1 13.2 %all-to-all-start.1 = ((bf16[3,32,8,128]{3,2,0,1:T(8,128)(2,1)}), bf16[3,32,8,128]{3,2,0,1:T(8,128)(2,1)S(1)}, u32[]{:S(2)}, u32[]{:S(2)}) async-start(bf16[3,32,8,128]{3,2,0,1:T(8,128)(2,1)} %slice.4), calls=%async_computation.1 | async-start | bytes 393216 | tf_op jit(solution)/shard_map/all_to_all | solution.py:81
  24.3 259.6 %while.26 = (s32[]{:T(128)}, bf16[30,32,8,128]{3,2,0,1:T(8,128)(2,1)}, s32[30]{0:T(128)S(1)}, bf16[3,32,8,384]{3,2,0,1:T(8,128)(2,1)S(1)}, s32[30]{0:T(128)S(1)}...) while((s32[]{:T(128)}, ...), condition=%wide.region_4.5_spmd, body=%wide.region_0.4_spmd.sunk | while | flops 25691788 | bytes 263137 | solution.py:77
  283.9 9.8 %all-to-all-start = ((bf16[30,32,8,128]{3,2,0,1:T(8,128)(2,1)}), bf16[30,32,8,128]{3,2,0,1:T(8,128)(2,1)S(1)}, u32[]{:S(2)}, u32[]{:S(2)}) async-start(bf16[30,32,8,128]{3,2,0,1:T(8,128)(2,1)} %get-tuple-element.184), calls=%async_computation | async-start | bytes 3932160 | tf_op jit(solution)/shard_map/all_to_all | solution.py:80
  293.8 48.5 %all-to-all-done = bf16[30,32,8,128]{3,2,0,1:T(8,128)(2,1)S(1)} async-done(((bf16[30,32,8,128]{3,2,0,1:T(8,128)(2,1)}), bf16[30,32,8,128]{3,2,0,1:T(8,128)(2,1)S(1)}, u32[]{:S(2)}, u32[]{:S(2)}) %all-to-all-start) | async-done | bytes 1966112 | tf_op jit(solution)/shard_map/all_to_all | solution.py:80
  342.3 1.8 copy.40
  344.2 388.2 %while.27 = (s32[]{:T(128)}, f32[30,1,256,128]{3,2,1,0:T(8,128)}, f32[30]{0:T(128)S(1)}, s32[30]{0:T(128)S(1)}, s32[30]{0:T(128)S(1)}, /*index=5*/f32[10]{0:T(12...) while((s32[]{:T(128)}, f32[30,1,256,128]{3,2,1,0:T(8,128)}, ...), condition=%wide.region_10.11_spmd, body=%wide.region_5.10_spmd.sunk | while | flops 17467012 | bytes 525359 | solution.py:93
  346.7 1.4 fusion.78
  351.9 1.8 bitcast_dynamic-update-slice_fusion.2
  359.6 1.4 fusion.78
  364.9 1.8 bitcast_dynamic-update-slice_fusion.2
  372.6 1.4 fusion.78
  377.8 1.8 bitcast_dynamic-update-slice_fusion.2
  385.5 1.4 fusion.78
  390.8 1.8 bitcast_dynamic-update-slice_fusion.2
  398.5 1.4 fusion.78
  403.7 1.8 bitcast_dynamic-update-slice_fusion.2
  411.4 1.4 fusion.78
  416.6 1.8 bitcast_dynamic-update-slice_fusion.2
  424.3 1.4 fusion.78
  429.6 1.8 bitcast_dynamic-update-slice_fusion.2
  437.3 1.4 fusion.78
  442.5 1.8 bitcast_dynamic-update-slice_fusion.2
  450.2 1.4 fusion.78
  455.5 1.8 bitcast_dynamic-update-slice_fusion.2
  468.4 1.8 bitcast_dynamic-update-slice_fusion.2
  476.1 1.4 fusion.78
  481.4 1.8 bitcast_dynamic-update-slice_fusion.2
  489.1 1.4 fusion.78
  494.3 1.8 bitcast_dynamic-update-slice_fusion.2
  502.0 1.4 fusion.78
  507.2 1.8 bitcast_dynamic-update-slice_fusion.2
  514.9 1.4 fusion.78
  520.2 1.8 bitcast_dynamic-update-slice_fusion.2
  533.1 1.8 bitcast_dynamic-update-slice_fusion.2
  546.0 1.8 bitcast_dynamic-update-slice_fusion.2
  553.8 1.4 fusion.78
  559.0 1.8 bitcast_dynamic-update-slice_fusion.2
  571.9 1.8 bitcast_dynamic-update-slice_fusion.2
  579.6 1.4 fusion.78
  584.9 1.8 bitcast_dynamic-update-slice_fusion.2
  597.8 1.8 bitcast_dynamic-update-slice_fusion.2
  610.8 1.8 bitcast_dynamic-update-slice_fusion.2
  623.7 1.8 bitcast_dynamic-update-slice_fusion.2
  636.6 1.8 bitcast_dynamic-update-slice_fusion.2
  644.3 1.4 fusion.78
  649.6 1.8 bitcast_dynamic-update-slice_fusion.2
  657.3 1.4 fusion.78
  662.5 1.8 bitcast_dynamic-update-slice_fusion.2
  670.2 1.4 fusion.78
  675.5 1.8 bitcast_dynamic-update-slice_fusion.2
  683.2 1.4 fusion.78
  688.4 1.8 bitcast_dynamic-update-slice_fusion.2
  696.1 1.4 fusion.78
  701.4 1.8 bitcast_dynamic-update-slice_fusion.2
  709.1 1.4 fusion.78
  714.3 1.8 bitcast_dynamic-update-slice_fusion.2
  722.0 1.4 fusion.78
  727.2 1.8 bitcast_dynamic-update-slice_fusion.2
  732.4 96.1 %psum.7 = f32[30]{0:T(128)S(1)} all-reduce(f32[30]{0:T(128)S(1)} %get-tuple-element.185), channel_id=1, replica_groups=mesh['row'=32,'col'=16] {'row','col'}, use_global_device_ids=true, to_apply=%region_11.12 | all-reduce | flops 30 | bytes 240 | tf_op jit(solution)/shard_map/psum | solution.py:97
  831.1 6.3 fusion.49
  837.8 20.4 %all_to_all.33 = f32[3,1,256,128]{3,1,0,2:T(1,128)S(1)} all-to-all(f32[3,1,256,128]{3,1,0,2:T(1,128)S(1)} %copy.26), channel_id=1, replica_groups=mesh['row'=32,'col'=16] {'row'}, dimensions={2} | all-to-all | bytes 786432 | tf_op jit(solution)/shard_map/all_to_all | solution.py:111
  (335 shorter events, 276.0 us)
Async XLA Ops:
  0.6 23.7 %copy-start.2 = (s32[30]{0:T(128)S(1)}, s32[30]{0:T(128)}, u32[]{:S(2)}) copy-start(s32[30]{0:T(128)} %param.10) | copy-start | bytes 364
  0.6 23.7 %copy-start.3 = (f32[10]{0:T(128)S(1)}, f32[10]{0:T(128)}, u32[]{:S(2)}) copy-start(f32[10]{0:T(128)} %param.11) | copy-start | bytes 124
  0.6 6.6 collective-permute-start
  2.7 6.5 collective-permute-start.1
  11.1 272.8 %all-to-all-start.1 = ((bf16[3,32,8,128]{3,2,0,1:T(8,128)(2,1)}), bf16[3,32,8,128]{3,2,0,1:T(8,128)(2,1)S(1)}, u32[]{:S(2)}, u32[]{:S(2)}) async-start(bf16[3,32,8,128]{3,2,0,1:T(8,128)(2,1)} %slice.4), calls=%async_computation.1 | async-start | bytes 393216 | tf_op jit(solution)/shard_map/all_to_all | solution.py:81
  283.9 58.4 %all-to-all-start = ((bf16[30,32,8,128]{3,2,0,1:T(8,128)(2,1)}), bf16[30,32,8,128]{3,2,0,1:T(8,128)(2,1)S(1)}, u32[]{:S(2)}, u32[]{:S(2)}) async-start(bf16[30,32,8,128]{3,2,0,1:T(8,128)(2,1)} %get-tuple-element.184), calls=%async_computation | async-start | bytes 3932160 | tf_op jit(solution)/shard_map/all_to_all | solution.py:80
  829.1 8.3 copy-start.1
  831.1 27.2 %copy-start = (f32[32,8,128]{2,1,0:T(8,128)S(1)}, f32[32,8,128]{2,1,0:T(8,128)}, u32[]{:S(2)}) copy-start(f32[32,8,128]{2,1,0:T(8,128)} %param.8) | copy-start | bytes 393220
where the time goes:
time: 866 us; the launch traced here: 859 us
  loops' own time  293 us (34%)
  other arithmetic  219 us (25%)
  blocking collectives  116 us (13%)
  matrix products  89.1 us (10%)
  local copies, waits for them, and re-layouts  60.6 us (7%)
  waiting for transfers between devices  50.7 us (6%)
  starting transfers between devices  28.6 us (3%)
    another operation x1, loops' own time, per_device(): smoothed, partials = lax.map(along_y, channel_ids)  174 us
    another operation x1, loops' own time, per_device(): panels = lax.map(partial(smooth_x, wide), channel_ids)  119 us
    psum x1, blocking collectives, per_device(): compliance = lax.psum(partials, ('row', 'col')) / cell_count  96.1 us
    reduce_sum x60, other arithmetic, width_of(): jnp.sum(jnp.where(jnp.arange(channel_width.shape[0]) == index, channel_wi...  80.9 us
    reduce_sum x60, other arithmetic, width_of(): jnp.sum(jnp.where(jnp.arange(sigma_table.shape[0]) == slot, sigma_table,...  75.4 us
    dot_general x30, matrix products, along_y(): jnp.einsum('zyx,yw->zwx', source, matrix, preferred_element_type=jnp.floa...  54.6 us
    all_to_all x1, waiting for transfers between devices, per_device(): lax.all_to_all(panels, 'row', split_axis=1, concat_axis=2, tiled=True)  48.5 us
    reduce_sum x60, other arithmetic, gauss_band(): jnp.sum(jnp.exp(-tap_axis * tap_axis / (2.0 * width_value * width_value)))  39.1 us
  transfers between devices with their start and end apart: 4, of which 3 were waited for; matrix products, arithmetic and copies ran while one was open for 16% of the time, Pallas kernels for 0%

commit v1 on v0

--- a/solution.py
+++ b/solution.py
@@ -1,8 +1,10 @@
+import functools
 from functools import partial
 import jax
 import jax.numpy as jnp
 from jax import lax
 from jax.sharding import PartitionSpec as P
+from jax.lax import all_gather
 
 VARIANTS = 3
 WIDTHS = 10
@@ -10,6 +12,13 @@
 HALF = 128
 sharpness = 8.0
 spread_floor = 0.0001
+
+
+def play_wall_now(view, lane_axis):
+    return jnp.sum(all_gather(view, axis_name=lane_axis), 0)
+
+
+track_matrix = functools.partial(play_wall_now, lane_axis=("row", "col"))
 
 
 def extended(x, sides, width):
@@ -94,7 +103,7 @@
     cell_count = (
         lax.axis_size("row") * lax.axis_size("col") * variants.shape[1] * length * variants.shape[3]
     )
-    compliance = lax.psum(partials, ("row", "col")) / cell_count
+    compliance = track_matrix(partials) / cell_count
     mean_value = jnp.mean(compliance)
     spread = jnp.sqrt(jnp.mean((compliance - mean_value) ** 2) + spread_floor)
     weights = (1.0 + (compliance - mean_value) / spread) / CHANNELS

time: 866 us -> 867 us (level)
    unnamed x0 -> x1, blocking collectives: none -> 96.4 us
    psum x1 -> x0, blocking collectives: 96.1 us -> none  [per_device(): compliance = lax.psum(partials, ('row', 'col')) / cell_count]
where the time goes in v1:
time: 867 us; the launch traced here: 860 us
  loops' own time  293 us (34%)
  other arithmetic  219 us (25%)
  blocking collectives  117 us (13%)
  matrix products  89.1 us (10%)
  local copies, waits for them, and re-layouts  61.1 us (7%)
  waiting for transfers between devices  50.7 us (6%)
  starting transfers between devices  28.6 us (3%)
    another operation x1, loops' own time, per_device(): smoothed, partials = lax.map(along_y, channel_ids)  174 us
    another operation x1, loops' own time, per_device(): panels = lax.map(partial(smooth_x, wide), channel_ids)  119 us
    unnamed x1, blocking collectives  96.4 us
    reduce_sum x60, other arithmetic, width_of(): jnp.sum(jnp.where(jnp.arange(channel_width.shape[0]) == index, channel_wi...  80.9 us
    reduce_sum x60, other arithmetic, width_of(): jnp.sum(jnp.where(jnp.arange(sigma_table.shape[0]) == slot, sigma_table,...  75.4 us
    dot_general x30, matrix products, along_y(): jnp.einsum('zyx,yw->zwx', source, matrix, preferred_element_type=jnp.floa...  54.6 us
    all_to_all x1, waiting for transfers between devices, per_device(): lax.all_to_all(panels, 'row', split_axis=1, concat_axis=2, tiled=True)  48.5 us
    reduce_sum x60, other arithmetic, gauss_band(): jnp.sum(jnp.exp(-tap_axis * tap_axis / (2.0 * width_value * width_value)))  39.1 us
  transfers between devices with their start and end apart: 4, of which 3 were waited for; matrix products, arithmetic and copies ran while one was open for 16% of the time, Pallas kernels for 0%

profile of v1, /device:TPU:16, one launch (start us, length us, event | category | flops | bytes accessed | tf_op | source)
XLA Modules:
  0.0 860.0 jit_solution(5085560956758222623)
XLA Ops:
  0.6 2.1 collective-permute-start
  2.7 3.6 collective-permute-start.1
  7.3 1.9 collective-permute-done.1
  11.1 13.2 %all-to-all-start.1 = ((bf16[3,32,8,128]{3,2,0,1:T(8,128)(2,1)}), bf16[3,32,8,128]{3,2,0,1:T(8,128)(2,1)S(1)}, u32[]{:S(2)}, u32[]{:S(2)}) async-start(bf16[3,32,8,128]{3,2,0,1:T(8,128)(2,1)} %slice.4), calls=%async_computation.1 | async-start | bytes 393216 | tf_op jit(solution)/shard_map/all_to_all | solution.py:90
  24.3 259.6 %while.26 = (s32[]{:T(128)}, bf16[30,32,8,128]{3,2,0,1:T(8,128)(2,1)}, s32[30]{0:T(128)S(1)}, bf16[3,32,8,384]{3,2,0,1:T(8,128)(2,1)S(1)}, s32[30]{0:T(128)S(1)}...) while((s32[]{:T(128)}, ...), condition=%wide.region_4.5_spmd, body=%wide.region_0.4_spmd.sunk | while | flops 25691788 | bytes 263137 | solution.py:86
  283.9 9.8 %all-to-all-start = ((bf16[30,32,8,128]{3,2,0,1:T(8,128)(2,1)}), bf16[30,32,8,128]{3,2,0,1:T(8,128)(2,1)S(1)}, u32[]{:S(2)}, u32[]{:S(2)}) async-start(bf16[30,32,8,128]{3,2,0,1:T(8,128)(2,1)} %get-tuple-element.184), calls=%async_computation | async-start | bytes 3932160 | tf_op jit(solution)/shard_map/all_to_all | solution.py:89
  293.8 48.5 %all-to-all-done = bf16[30,32,8,128]{3,2,0,1:T(8,128)(2,1)S(1)} async-done(((bf16[30,32,8,128]{3,2,0,1:T(8,128)(2,1)}), bf16[30,32,8,128]{3,2,0,1:T(8,128)(2,1)S(1)}, u32[]{:S(2)}, u32[]{:S(2)}) %all-to-all-start) | async-done | bytes 1966112 | tf_op jit(solution)/shard_map/all_to_all | solution.py:89
  342.3 1.8 copy.41
  344.2 388.2 %while.27 = (s32[]{:T(128)}, f32[30,1,256,128]{3,2,1,0:T(8,128)}, f32[30]{0:T(128)S(1)}, s32[30]{0:T(128)S(1)}, s32[30]{0:T(128)S(1)}, /*index=5*/f32[10]{0:T(12...) while((s32[]{:T(128)}, f32[30,1,256,128]{3,2,1,0:T(8,128)}, ...), condition=%wide.region_10.11_spmd, body=%wide.region_5.10_spmd.sunk | while | flops 17467012 | bytes 525359 | solution.py:102
  346.7 1.4 fusion.78
  351.9 1.8 bitcast_dynamic-update-slice_fusion.2
  359.6 1.4 fusion.78
  364.9 1.8 bitcast_dynamic-update-slice_fusion.2
  372.6 1.4 fusion.78
  377.8 1.8 bitcast_dynamic-update-slice_fusion.2
  385.5 1.4 fusion.78
  390.7 1.8 bitcast_dynamic-update-slice_fusion.2
  398.5 1.4 fusion.78
  403.7 1.8 bitcast_dynamic-update-slice_fusion.2
  411.4 1.4 fusion.78
  416.6 1.8 bitcast_dynamic-update-slice_fusion.2
  424.3 1.4 fusion.78
  429.6 1.8 bitcast_dynamic-update-slice_fusion.2
  437.3 1.4 fusion.78
  442.5 1.8 bitcast_dynamic-update-slice_fusion.2
  450.2 1.4 fusion.78
  455.5 1.8 bitcast_dynamic-update-slice_fusion.2
  463.2 1.4 fusion.78
  468.4 1.8 bitcast_dynamic-update-slice_fusion.2
  476.1 1.4 fusion.78
  481.3 1.8 bitcast_dynamic-update-slice_fusion.2
  489.1 1.4 fusion.78
  494.3 1.8 bitcast_dynamic-update-slice_fusion.2
  502.0 1.4 fusion.78
  507.2 1.8 bitcast_dynamic-update-slice_fusion.2
  514.9 1.4 fusion.78
  520.2 1.8 bitcast_dynamic-update-slice_fusion.2
  527.9 1.4 fusion.78
  533.1 1.8 bitcast_dynamic-update-slice_fusion.2
  546.0 1.8 bitcast_dynamic-update-slice_fusion.2
  559.0 1.8 bitcast_dynamic-update-slice_fusion.2
  566.7 1.4 fusion.78
  571.9 1.8 bitcast_dynamic-update-slice_fusion.2
  579.6 1.4 fusion.78
  584.9 1.8 bitcast_dynamic-update-slice_fusion.2
  597.8 1.8 bitcast_dynamic-update-slice_fusion.2
  605.5 1.4 fusion.78
  610.8 1.8 bitcast_dynamic-update-slice_fusion.2
  623.7 1.8 bitcast_dynamic-update-slice_fusion.2
  636.6 1.8 bitcast_dynamic-update-slice_fusion.2
  644.3 1.4 fusion.78
  649.6 1.8 bitcast_dynamic-update-slice_fusion.2
  657.3 1.4 fusion.78
  662.5 1.8 bitcast_dynamic-update-slice_fusion.2
  675.5 1.8 bitcast_dynamic-update-slice_fusion.2
  688.4 1.8 bitcast_dynamic-update-slice_fusion.2
  696.1 1.4 fusion.78
  701.4 1.8 bitcast_dynamic-update-slice_fusion.2
  709.1 1.4 fusion.78
  714.3 1.8 bitcast_dynamic-update-slice_fusion.2
  727.2 1.8 bitcast_dynamic-update-slice_fusion.2
  732.7 96.4 %all-reduce = f32[15360]{0:T(1024)S(1)} all-reduce(f32[15360]{0:T(1024)S(1)} %dynamic-update-slice), channel_id=2, replica_groups=mesh['row'=32,'col'=16] {'row','col'}, use_global_device_ids=true, to_apply=%add | all-reduce | flops 15360 | bytes 122880
  832.0 6.3 fusion.49
  838.7 20.5 %all_to_all.33 = f32[3,1,256,128]{3,1,0,2:T(1,128)S(1)} all-to-all(f32[3,1,256,128]{3,1,0,2:T(1,128)S(1)} %copy.27), channel_id=1, replica_groups=mesh['row'=32,'col'=16] {'row'}, dimensions={2} | all-to-all | bytes 786432 | tf_op jit(solution)/shard_map/all_to_all | solution.py:120
  (339 shorter events, 276.6 us)
Async XLA Ops:
  0.6 23.7 %copy-start.2 = (s32[30]{0:T(128)S(1)}, s32[30]{0:T(128)}, u32[]{:S(2)}) copy-start(s32[30]{0:T(128)} %param.10) | copy-start | bytes 364
  0.6 23.7 %copy-start.3 = (f32[10]{0:T(128)S(1)}, f32[10]{0:T(128)}, u32[]{:S(2)}) copy-start(f32[10]{0:T(128)} %param.11) | copy-start | bytes 124
  0.6 6.6 collective-permute-start
  2.7 6.5 collective-permute-start.1
  11.1 272.8 %all-to-all-start.1 = ((bf16[3,32,8,128]{3,2,0,1:T(8,128)(2,1)}), bf16[3,32,8,128]{3,2,0,1:T(8,128)(2,1)S(1)}, u32[]{:S(2)}, u32[]{:S(2)}) async-start(bf16[3,32,8,128]{3,2,0,1:T(8,128)(2,1)} %slice.4), calls=%async_computation.1 | async-start | bytes 393216 | tf_op jit(solution)/shard_map/all_to_all | solution.py:90
  283.9 58.4 %all-to-all-start = ((bf16[30,32,8,128]{3,2,0,1:T(8,128)(2,1)}), bf16[30,32,8,128]{3,2,0,1:T(8,128)(2,1)S(1)}, u32[]{:S(2)}, u32[]{:S(2)}) async-start(bf16[30,32,8,128]{3,2,0,1:T(8,128)(2,1)} %get-tuple-element.184), calls=%async_computation | async-start | bytes 3932160 | tf_op jit(solution)/shard_map/all_to_all | solution.py:89
  830.0 8.3 copy-start.1
  832.0 27.2 %copy-start = (f32[32,8,128]{2,1,0:T(8,128)S(1)}, f32[32,8,128]{2,1,0:T(8,128)}, u32[]{:S(2)}) copy-start(f32[32,8,128]{2,1,0:T(8,128)} %param.8) | copy-start | bytes 393220
